TPU v7x, 256 devices: a whole 4x4x8 slice. The times are simulated.
256 devices in a mesh: row: 32 (over y_hi, z, core), col: 8 (over x, y_lo).
Axes of the slice: x: 4, y: 4 (y_hi: 2, y_lo: 2; y = y_hi * 2 + y_lo), z: 8, core: 2. Of those that a mesh axis runs over, the one named last changes fastest.
Arguments:
- pair: bfloat16 [512, 512, 128], P('row', 'col'), may hold values from -6 to 6
- in_gain: float32 [2, 128], replicated, may hold values from 0.25 to 1.75
- in_bias: float32 [2, 128], replicated, may hold values from -2 to 2
- projection: bfloat16 [2, 128, 640], replicated, may hold values from -0.5 to 0.5
- out_gain: float32 [2, 128], replicated, may hold values from 0.25 to 1.75
- out_bias: float32 [2, 128], replicated, may hold values from -2 to 2
- out_weight: bfloat16 [2, 128, 128], replicated, may hold values from -0.5 to 0.5
Outputs:
- updated: bfloat16 [512, 512, 128], P('row', 'col')
All inputs are finite; a program needn't handle non-finite values.
Results may differ from a plain program's by a relative error of at most 0.014.
Values may be sent and summed in bfloat16 or wider, within the bound.
A program may use at most 64 MiB of HBM per device.

v0:
```python
import jax
import jax.numpy as jnp
from jax import lax
from jax.sharding import PartitionSpec as P


def layer_norm(values, gain, offset):
    mean = jnp.mean(values, axis=-1, keepdims=True)
    centred = values - mean
    var = jnp.mean(centred * centred, axis=-1, keepdims=True)
    return centred / jnp.sqrt(var + 1e-05) * gain + offset


def project_tile(state, which, in_gain, in_bias, projection):
    rows, cols, chans = state.shape
    hidden = (projection.shape[2] - chans) // 4
    normed = layer_norm(state.astype(jnp.float32), in_gain[which], in_bias[which]).astype(
        jnp.bfloat16
    )
    proj = jnp.dot(
        normed.reshape(rows * cols, chans), projection[which], preferred_element_type=jnp.float32
    )
    left = (jax.nn.sigmoid(proj[:, hidden : 2 * hidden]) * proj[:, :hidden]).astype(jnp.bfloat16)
    right = (
        jax.nn.sigmoid(proj[:, 3 * hidden : 4 * hidden]) * proj[:, 2 * hidden : 3 * hidden]
    ).astype(jnp.bfloat16)
    gate = jax.nn.sigmoid(proj[:, 4 * hidden :])
    return (left.reshape(rows, cols, hidden), right.reshape(rows, cols, hidden), gate)


def finish_tile(state, tri, gate, which, out_gain, out_bias, out_weight):
    rows, cols, chans = state.shape
    hidden = tri.shape[2]
    normtri = layer_norm(tri, out_gain[which], out_bias[which]).astype(jnp.bfloat16)
    delta = jnp.dot(
        normtri.reshape(rows * cols, hidden), out_weight[which], preferred_element_type=jnp.float32
    )
    result = state.astype(jnp.float32).reshape(rows * cols, chans) + gate * delta
    return result.astype(jnp.bfloat16).reshape(rows, cols, chans)


def local(pair, in_gain, in_bias, projection, out_gain, out_bias, out_weight):
    left, right, gate = project_tile(pair, 0, in_gain, in_bias, projection)
    strip = lax.all_gather(right, "row", axis=0, tiled=True)
    mirrored = lax.all_to_all(strip, "col", split_axis=0, concat_axis=1, tiled=True)
    partner = mirrored
    tri = jnp.einsum(
        "ikh,jkh->ijh",
        lax.all_gather(left, "col", axis=1, tiled=True),
        partner,
        preferred_element_type=jnp.float32,
    )
    state1 = finish_tile(pair, tri, gate, 0, out_gain, out_bias, out_weight)
    left, right, gate = project_tile(state1, 1, in_gain, in_bias, projection)
    strip = lax.all_gather(left, "col", axis=1, tiled=True)
    mirrored = lax.all_to_all(strip, "row", split_axis=1, concat_axis=0, tiled=True)
    partner = mirrored
    tri = jnp.einsum(
        "kih,kjh->ijh",
        partner,
        lax.all_gather(right, "row", axis=0, tiled=True),
        preferred_element_type=jnp.float32,
    )
    return finish_tile(state1, tri, gate, 1, out_gain, out_bias, out_weight)


def solution(mesh):
    return jax.shard_map(
        local,
        mesh=mesh,
        in_specs=(P("row", "col", None), P(), P(), P(), P(), P(), P()),
        out_specs=P("row", "col", None),
        check_vma=False,
    )
```

profile of v0, /device:TPU:1, one launch (start us, length us, event | category | flops | bytes accessed | tf_op | source)
XLA Modules:
  0.0 552.3 jit_solution(13216614345364434626)
XLA Ops:
  7.4 0.0 all-gather.5.cloned.1.call-start
  7.4 1.2 convert_reduce_fusion
  8.5 1.3 multiply_reduce_fusion.3
  9.9 0.8 slice_bitcast_fusion.2
  10.7 1.3 add_convert_fusion.3
  12.0 1.4 fusion.33
  13.4 1.0 fusion.16
  14.4 0.0 all-gather.5.cloned.1.call-update
  14.4 0.0 copy-start.3
  14.4 0.0 copy-start.4
  14.4 105.8 %all-gather.5.cloned.1.call-done = bf16[512,64,128]{2,1,0:T(8,128)(2,1)} async-done(((bf16[16,64,128]{2,1,0:T(8,128)(2,1)}), bf16[512,64,128]{2,1,0:T(8,128)(2,1)}) %all-gather.5.cloned.1.call-update) | async-done | bytes 8388624 | tf_op jit(solution)/shard_map/all_gather | solution.py:44
  120.2 4.9 all-to-all-start
  125.1 0.0 all-gather.7.cloned.1.call-start
  125.2 0.9 copy.38
  126.1 0.0 all-gather.7.cloned.1.call-update
  126.1 0.0 all-gather.11.cloned.1.call-start
  126.1 0.0 copy-done.3
  126.2 0.0 copy-done.4
  126.2 134.4 %all-gather.7.cloned.1.call-done = bf16[16,512,128]{2,0,1:T(8,128)(2,1)} async-done(((bf16[16,64,128]{2,0,1:T(8,128)(2,1)}), bf16[16,512,128]{2,0,1:T(8,128)(2,1)}) %all-gather.7.cloned.1.call-update) | async-done | bytes 2097168 | tf_op jit(solution)/shard_map/all_gather | solution.py:49
  260.6 4.9 copy.40
  265.5 0.0 all-to-all-done
  265.5 9.6 %copy.37 = bf16[64,8,64,128]{3,2,1,0:T(8,128)(2,1)} copy(bf16[64,8,64,128]{3,2,0,1:T(8,128)(2,1)} %bitcast.7) | data formatting | bytes 16777216 | tf_op jit(solution)/shard_map/all_to_all | solution.py:45
  275.1 12.6 %copy.39 = bf16[64,512,128]{1,0,2:T(8,128)(2,1)} copy(bf16[64,512,128]{2,1,0:T(8,128)(2,1)} %bitcast.59) | data formatting | bytes 16777216 | tf_op jit(solution)/shard_map/all_to_all | solution.py:45
  287.7 6.3 %fusion.41 = (f32[16,64]{1,0:T(8,128)S(1)}, f32[16,64,128]{1,0,2:T(8,128)S(1)}) fusion(bf16[64,512,128]{1,0,2:T(8,128)(2,1)} %copy.39, bf16[16,512,128]{1,0,2:T(8,128)(2,1)} %copy.40), kind=kOutput, calls=%fused_computation.80 | convolution fusion | flops 134347776 | bytes 11014144 | tf_op jit(solution)/shard_map/ikh,jkh->ijh/dot_general | solution.py:47
  294.0 0.2 multiply_reduce_fusion.1
  294.2 0.3 add_convert_fusion.1
  294.6 1.1 copy.41
  295.7 1.4 fusion.42
  297.1 0.4 multiply_reduce_fusion.2
  297.5 0.6 fusion.27
  298.1 0.0 copy-start
  298.1 1.5 copy-done
  299.6 0.3 fusion.5
  299.9 0.9 copy.43
  300.8 0.0 all-gather.11.cloned.1.call-update
  300.8 0.0 all-gather.9.cloned.1.call-start
  300.8 1.2 copy.42
  302.0 0.0 all-gather.9.cloned.1.call-update
  302.1 48.4 %all-gather.11.cloned.1.call-done = bf16[16,512,128]{2,0,1:T(8,128)(2,1)} async-done(((bf16[16,64,128]{2,0,1:T(8,128)(2,1)}), bf16[16,512,128]{2,0,1:T(8,128)(2,1)}) %all-gather.11.cloned.1.call-update) | async-done | bytes 2097168 | tf_op jit(solution)/shard_map/all_gather | solution.py:55
  350.5 73.8 %all_to_all.36 = bf16[16,512,128]{2,0,1:T(8,128)(2,1)S(1)} all-to-all(bf16[16,512,128]{2,0,1:T(8,128)(2,1)} %all-gather.11.cloned.1.call-done), channel_id=1, replica_groups=mesh['row'=32,'col'=8] {'row'}, dimensions={1} | all-to-all | bytes 4194304 | tf_op jit(solution)/shard_map/all_to_all | solution.py:56
  424.3 1.9 copy.45
  426.1 3.9 copy.46
  430.1 104.6 %all-gather.9.cloned.1.call-done = bf16[512,64,128]{1,0,2:T(8,128)(2,1)} async-done(((bf16[16,64,128]{1,0,2:T(8,128)(2,1)}), bf16[512,64,128]{1,0,2:T(8,128)(2,1)}) %all-gather.9.cloned.1.call-update) | async-done | bytes 8388624 | tf_op jit(solution)/shard_map/all_gather | solution.py:61
  534.6 7.0 %fusion.43 = (f32[16,64]{1,0:T(8,128)S(1)}, f32[16,64,128]{1,0,2:T(8,128)S(1)}) fusion(bf16[512,16,128]{0,1,2:T(8,128)(2,1)S(1)} %copy.46, bf16[512,64,128]{1,0,2:T(8,128)(2,1)} %all-gather.9.cloned.1.call-done), kind=kOutput, calls=%fused_computation.82 | convolution fusion | flops 134347776 | bytes 11014144 | tf_op jit(solution)/shard_map/kih,kjh->ijh/dot_general | solution.py:58
  541.7 0.2 multiply_reduce_fusion
  541.9 0.3 add_convert_fusion
  542.2 0.5 copy.47
  542.7 2.0 fusion.2
  (15 shorter events, 0.1 us)
Async XLA Ops:
  7.4 112.8 %all-gather.5.cloned.1.call-start = ((), (), s32[]{:S(2)}) async-start(), calls=%async_computation.2 | async-start | bytes 8650752 | tf_op jit(solution)/shard_map/all_gather | solution.py:44
  14.4 111.8 %copy-start.3 = (f32[2,128]{1,0:T(2,128)S(1)}, f32[2,128]{1,0:T(2,128)}, u32[]{:S(2)}) copy-start(f32[2,128]{1,0:T(2,128)} %param.12) | copy-start | bytes 3076
  14.4 111.8 %copy-start.4 = (f32[2,128]{1,0:T(2,128)S(1)}, f32[2,128]{1,0:T(2,128)}, u32[]{:S(2)}) copy-start(f32[2,128]{1,0:T(2,128)} %param.11) | copy-start | bytes 3076
  120.2 145.3 %all-to-all-start = ((bf16[512,64,128]{2,1,0:T(8,128)(2,1)}), bf16[512,64,128]{2,1,0:T(8,128)(2,1)}, u32[]{:S(2)}, u32[]{:S(2)}) async-start(bf16[512,64,128]{2,1,0:T(8,128)(2,1)} %all-gather.5.cloned.1.call-done), calls=%async_computation | async-start | bytes 16777216 | tf_op jit(solution)/shard_map/all_to_all | solution.py:45
  125.1 135.4 %all-gather.7.cloned.1.call-start = ((), (), s32[]{:S(2)}) async-start(), calls=%async_computation.3 | async-start | bytes 2359296 | tf_op jit(solution)/shard_map/all_gather | solution.py:49
  126.1 224.4 %all-gather.11.cloned.1.call-start = ((), (), s32[]{:S(2)}) async-start(), calls=%async_computation.5 | async-start | bytes 2359296 | tf_op jit(solution)/shard_map/all_gather | solution.py:55
  294.0 1.7 copy-start.1
  294.0 1.7 copy-start.5
  295.7 1.8 copy-start.2
  298.1 1.5 copy-start
  300.8 233.8 %all-gather.9.cloned.1.call-start = ((), (), s32[]{:S(2)}) async-start(), calls=%async_computation.4 | async-start | bytes 17301504 | tf_op jit(solution)/shard_map/all_gather | solution.py:61
Sparse Core Ops, SparseCore 0:
  14.5 105.6 all-gather.4
Sparse Core Ops, SparseCore 1:
  127.4 133.1 all-gather.6
  300.9 49.6 all-gather.10
  352.9 181.6 all-gather.8
where the time goes:
time: 553 us; the launch traced here: 552 us
  waiting for transfers between devices  393 us (71%)
  blocking collectives  73.8 us (13%)
  local copies, waits for them, and re-layouts  39.8 us (7%)
  matrix products  18.7 us (3%)
  between operations  15.2 us (3%)
  other arithmetic  6.54 us (1%)
    all_gather x1, waiting for transfers between devices, local(): lax.all_gather(left, 'col', axis=1, tiled=True)  134 us
    all_gather x1, waiting for transfers between devices, local(): strip = lax.all_gather(right, 'row', axis=0, tiled=True)  106 us
    all_gather x1, waiting for transfers between devices, local(): lax.all_gather(right, 'row', axis=0, tiled=True)  105 us
    all_to_all x1, blocking collectives, local(): lax.all_to_all(strip, 'row', split_axis=1, concat_axis=0, tiled=True)  73.8 us
    all_gather x1, waiting for transfers between devices, local(): strip = lax.all_gather(left, 'col', axis=1, tiled=True)  48.4 us
    all_to_all x2, local copies, waits for them, and re-layouts, local(): lax.all_to_all(strip, 'col', split_axis=0, concat_axis=1, tiled=True)  22.2 us
  transfers between devices with their start and end apart: 5, of which 4 were waited for; matrix products, arithmetic and copies ran while one was open for 2% of the time, Pallas kernels for 0%

commit v1 on v0

v1 whole, which is shorter than its diff:
```python
import jax
import jax.numpy as jnp
from jax import lax
from jax.experimental import pallas as pl
from jax.experimental.pallas import tpu as pltpu
from jax.sharding import PartitionSpec as P

F32 = jnp.float32
BF16 = jnp.bfloat16
C = 128
H = 128
ROWS = 16
COLS = 64
LANES = ROWS * COLS
NZ = 8
NP = 16
GROUP = 2
NG = NZ // GROUP
STEPS = (0, 1, 7, 2, 6, 3, 5, 4)
BACK = (4, 3, 5, 2, 6, 1, 7, 0)
EPS = 1e-05


def column(row):
    eye = lax.broadcasted_iota(jnp.int32, (C, C), 0) == lax.broadcasted_iota(jnp.int32, (C, C), 1)
    return jnp.sum(jnp.where(eye, jnp.broadcast_to(row, (C, C)), 0.0), axis=1, keepdims=True)


def norm0(values, gain, offset):
    mean = jnp.sum(values, axis=0, keepdims=True) * (1.0 / C)
    centred = values - mean
    var = jnp.sum(centred * centred, axis=0, keepdims=True) * (1.0 / C)
    return centred * lax.rsqrt(var + EPS) * gain + offset


def sigmoid(x):
    return 0.5 * jnp.tanh(0.5 * x) + 0.5


def dot(a, b, dims):
    return lax.dot_general(a, b, (dims, ((), ())), preferred_element_type=F32)


def kernel(
    pair, in_gain, in_bias, projection, out_gain, out_bias, out_weight, updated,
    state, normed, gate, cols, wt, wo,
    sa, ra, spread, sx, rx, am, at, bm, tx, ty, tz, tf,
    s1, r1, s2, r2, s3, r3, s4, r4, s5, r5,
):
    row = lax.axis_index("row")
    col = lax.axis_index("col")
    core = row % 2
    z = (row // 2) % NZ
    yh = row // (2 * NZ)
    p = col * 2 + yh

    def zdev(zz):
        return ((yh * NZ + zz) * 2 + core, col)

    def pdev(pp):
        return (((pp % 2) * NZ + z) * 2 + core, pp // 2)

    sibling = (row - core + (1 - core), col)

    barrier = pltpu.get_barrier_semaphore()

    def greet_z(d, _):
        pl.semaphore_signal(barrier, 1, device_id=zdev((z + d) % NZ), device_id_type=pl.DeviceIdType.MESH)
        return 0

    def greet_p(d, _):
        pl.semaphore_signal(barrier, 1, device_id=pdev((p + d) % NP), device_id_type=pl.DeviceIdType.MESH)
        return 0

    lax.fori_loop(1, NZ, greet_z, 0)
    lax.fori_loop(1, NP, greet_p, 0)
    pl.semaphore_signal(barrier, 1, device_id=sibling, device_id_type=pl.DeviceIdType.MESH)

    def remote(src, dst, send, recv, device):
        return pltpu.make_async_remote_copy(
            src_ref=src, dst_ref=dst, send_sem=send, recv_sem=recv,
            device_id=device, device_id_type=pl.DeviceIdType.MESH,
        )

    low = lax.broadcasted_iota(jnp.int32, (1, 128), 1) < COLS

    def swap(x):
        return pltpu.roll(x, COLS, 1)

    for t in range(8):
        tile = jnp.concatenate([pair[t], pair[t + 8]], axis=0).astype(F32)
        state[:, t * 128:(t + 1) * 128] = tile.T
    for u in range(2):
        for n, ref in enumerate((in_gain, in_bias, out_gain, out_bias)):
            cols[u, n] = jnp.broadcast_to(column(ref[u:u + 1, :]), (C, 128))
        for g in range(5):
            wt[u, g * 128:(g + 1) * 128, :] = projection[u, :, g * 128:(g + 1) * 128].astype(F32).T.astype(BF16)
        wo[u] = out_weight[u].astype(F32).T.astype(BF16)

    pl.semaphore_wait(barrier, NZ - 1 + NP - 1 + 1)

    for u in range(2):
        def project(t, _):
            lanes = pl.ds(pl.multiple_of(t * 128, 128), 128)
            nrm = norm0(state[:, lanes], cols[u, 0], cols[u, 1]).astype(BF16)
            normed[:, lanes] = nrm
            proj = dot(wt[u, :512, :], nrm, ((1,), (0,)))
            left = (sigmoid(proj[128:256]) * proj[:128]).astype(BF16)
            right = (sigmoid(proj[384:512]) * proj[256:384]).astype(BF16)
            sa[u, :, 0:16, lanes] = left.reshape(NZ, 16, 128)
            sa[u, :, 16:32, lanes] = right.reshape(NZ, 16, 128)
            return 0

        lax.fori_loop(0, 8, project, 0)

        for d in (4, 3, 5, 2, 6, 1, 7):
            to = (z + d) % NZ
            remote(sa.at[u, to], ra.at[u, z], s1.at[u, d], r1.at[u, z], zdev(to)).start()

        def gates(t, _):
            lanes = pl.ds(pl.multiple_of(t * 128, 128), 128)
            gate[:, lanes] = sigmoid(dot(wt[u, 512:, :], normed[:, lanes], ((1,), (0,))))
            return 0

        lax.fori_loop(0, 8, gates, 0)

        def spread_out(s):
            zs = (z + STEPS[s]) % NZ
            if s > 0:
                remote(sa.at[u, zs], ra.at[u, zs], s1.at[u, 0], r1.at[u, zs], zdev(zs)).wait_recv()
            src = sa.at[u, zs] if s == 0 else ra.at[u, zs]
            for t in range(8):
                vl = src[0:16, t * 128:(t + 1) * 128].astype(F32)
                vr = src[16:32, t * 128:(t + 1) * 128].astype(F32)
                spread[pl.ds(t, 16, stride=16), :] = jnp.where(low, vl, swap(vr))
                spread[pl.ds(8 + t, 16, stride=16), :] = jnp.where(low, swap(vl), vr)
            sx[u, :, s] = spread[...].reshape(NP, 16, 128).astype(BF16)

        def send_plane(g):
            steps = pl.ds(g * GROUP, GROUP)
            pltpu.make_async_copy(sx.at[u, p, steps], rx.at[u, col, yh, core, steps], r2.at[u, g]).start()

            def one(d, _):
                to = (p + d) % NP
                remote(sx.at[u, to, steps], rx.at[u, col, yh, core, steps], s2.at[u, g], r2.at[u, g], pdev(to)).start()
                return 0

            lax.fori_loop(1, NP, one, 0)

        def swap_cores(g):
            steps = pl.ds(g * GROUP, GROUP)
            whole = rx.at[u, :, :, core, steps]
            pltpu.make_async_copy(whole, whole, r2.at[u, g]).wait()
            remote(whole, whole, s3.at[u, g], r3.at[u, g], sibling).start()

        def build(g):
            steps = pl.ds(g * GROUP, GROUP)
            other = rx.at[u, :, :, 1 - core, steps]
            pltpu.make_async_copy(other, other, r3.at[u, g]).wait()
            for s in range(g * GROUP, (g + 1) * GROUP):
                zs = (z + STEPS[s]) % NZ
                for h in range(2):
                    for k in range(2):
                        place = pl.ds(pl.multiple_of(((h * NZ + zs) * 2 + k) * 16, 16), 16)
                        for c in range(4):
                            x0 = rx[u, 2 * c, h, k, s].astype(F32)
                            x1 = rx[u, 2 * c + 1, h, k, s].astype(F32)
                            am[place, c * 128:(c + 1) * 128] = jnp.where(low, x0, swap(x1)).astype(BF16)
                            bm[place, c * 128:(c + 1) * 128] = jnp.where(low, swap(x0), x1).astype(BF16)

        for g in range(NG):
            for s in range(g * GROUP, (g + 1) * GROUP):
                spread_out(s)
            send_plane(g)
            if g > 0:
                swap_cores(g - 1)
            if g > 1:
                build(g - 2)
        swap_cores(NG - 1)
        build(NG - 2)
        build(NG - 1)

        if u == 1:
            def flip(i, _):
                lanes = pl.ds(pl.multiple_of(i * 128, 128), 128)
                for k in range(4):
                    at[lanes, k * 128:(k + 1) * 128] = am[k * 128:(k + 1) * 128, lanes].astype(F32).T.astype(BF16)
                return 0

            lax.fori_loop(0, 4, flip, 0)
        a_ref = am if u == 0 else at

        def triangle(g):
            rows = []
            for s in BACK[g * GROUP:(g + 1) * GROUP]:
                for h in range(2):
                    r = ((h * NZ + (z + s) % NZ) * 2 + core) * 16
                    rows.append(a_ref[pl.ds(pl.multiple_of(r, 16), 16), :])
            tri = dot(jnp.concatenate(rows, axis=0), bm[...], ((1,), (1 - u,)))
            for h in range(2):
                for c in range(4):
                    first, second = [], []
                    for s in range(GROUP):
                        block = tri[(s * 2 + h) * 16:(s * 2 + h + 1) * 16, c * 128:(c + 1) * 128]
                        first.append(jnp.where(low, block[0:8], swap(block[8:16])))
                        second.append(jnp.where(low, swap(block[0:8]), block[8:16]))
                    tx[u, g, 4 * c + h] = jnp.concatenate(first, axis=0).astype(BF16)
                    tx[u, g, 4 * c + 2 + h] = jnp.concatenate(second, axis=0).astype(BF16)

        def send_back(g):
            pltpu.make_async_copy(tx.at[u, g, p], ty.at[u, g, p], r4.at[u, g]).start()

            def one(d, _):
                to = (p + d) % NP
                remote(tx.at[u, g, to], ty.at[u, g, p], s4.at[u, g], r4.at[u, g], pdev(to)).start()
                return 0

            lax.fori_loop(1, NP, one, 0)

        def gather_back(g):
            whole = ty.at[u, g]
            pltpu.make_async_copy(whole, whole, r4.at[u, g]).wait()
            for h in range(NP):
                spread[pl.ds(h, 16, stride=16), :] = ty[u, g, h].astype(F32)
            for n in range(GROUP):
                d = BACK[g * GROUP + n]
                for t in range(8):
                    at_row = (n * 8 + t) * 16
                    tile = spread[at_row:at_row + 16, :].astype(BF16)
                    if d == 0:
                        tf[u, z, :, t * 128:(t + 1) * 128] = tile
                    else:
                        tz[u, d, :, t * 128:(t + 1) * 128] = tile
                if d:
                    remote(tz.at[u, d], tf.at[u, z], s5.at[u, d], r5.at[u, z], zdev((z + d) % NZ)).start()

        for g in range(NG):
            triangle(g)
            send_back(g)
            if g > 0:
                gather_back(g - 1)
        gather_back(NG - 1)

        for d in range(1, NZ):
            zs = (z + d) % NZ
            remote(tz.at[u, d], tf.at[u, zs], s5.at[u, d], r5.at[u, zs], zdev(zs)).wait_recv()

        def finish(t, _):
            lanes = pl.ds(pl.multiple_of(t * 128, 128), 128)
            tri = tf[u, :, :, lanes].reshape(H, 128).astype(F32)
            nrm = norm0(tri, cols[u, 2], cols[u, 3]).astype(BF16)
            delta = dot(wo[u], nrm, ((1,), (0,)))
            new = state[:, lanes] + gate[:, lanes] * delta
            if u == 0:
                state[:, lanes] = new.astype(BF16).astype(F32)
            else:
                tile = new.T.astype(BF16)
                updated[t] = tile[0:COLS]
                updated[t + 8] = tile[COLS:]
            return 0

        lax.fori_loop(0, 8, finish, 0)

    for u in range(2):
        for d in range(1, NZ):
            zs = (z + d) % NZ
            remote(sa.at[u, zs], ra.at[u, z], s1.at[u, d], r1.at[u, z], zdev(zs)).wait_send()
            remote(tz.at[u, d], tf.at[u, z], s5.at[u, d], r5.at[u, z], zdev(zs)).wait_send()
        for g in range(NG):
            sent = sx.at[u, pl.ds(0, NP - 1), pl.ds(g * GROUP, GROUP)]
            pltpu.make_async_copy(sent, sent, s2.at[u, g]).wait()
            sent = tx.at[u, g, pl.ds(0, NP - 1)]
            pltpu.make_async_copy(sent, sent, s4.at[u, g]).wait()
            sent = rx.at[u, :, :, core, pl.ds(g * GROUP, GROUP)]
            pltpu.make_async_copy(sent, sent, s3.at[u, g]).wait()


def local(pair, in_gain, in_bias, projection, out_gain, out_bias, out_weight):
    vm = pltpu.VMEM
    dma = pltpu.SemaphoreType.DMA
    return pl.pallas_call(
        kernel,
        out_shape=jax.ShapeDtypeStruct((ROWS, COLS, C), BF16),
        in_specs=[pl.BlockSpec(memory_space=vm)] * 7,
        out_specs=pl.BlockSpec(memory_space=vm),
        scratch_shapes=[
            vm((C, LANES), F32),
            vm((C, LANES), BF16),
            vm((C, LANES), F32),
            vm((2, 4, C, 128), F32),
            vm((2, 640, C), BF16),
            vm((2, C, H), BF16),
            vm((2, NZ, 32, LANES), BF16),
            vm((2, NZ, 32, LANES), BF16),
            vm((256, 128), F32),
            vm((2, NP, NZ, 16, 128), BF16),
            vm((2, 8, 2, 2, NZ, 16, 128), BF16),
            vm((512, 512), BF16),
            vm((512, 512), BF16),
            vm((512, 512), BF16),
            vm((2, NG, NP, 16, 128), BF16),
            vm((2, NG, NP, 16, 128), BF16),
            vm((2, NZ, 16, LANES), BF16),
            vm((2, NZ, 16, LANES), BF16),
            dma((2, NZ)), dma((2, NZ)),
            dma((2, NG)), dma((2, NG)),
            dma((2, NG)), dma((2, NG)),
            dma((2, NG)), dma((2, NG)),
            dma((2, NZ)), dma((2, NZ)),
        ],
        compiler_params=pltpu.CompilerParams(
            collective_id=0, has_side_effects=True, vmem_limit_bytes=40 * 1024 * 1024
        ),
    )(pair, in_gain, in_bias, projection, out_gain, out_bias, out_weight)


def solution(mesh):
    return jax.shard_map(
        local,
        mesh=mesh,
        in_specs=(P("row", "col", None), P(), P(), P(), P(), P(), P()),
        out_specs=P("row", "col", None),
        check_vma=False,
    )
```

time: 553 us -> 106 us (0.19)
  waiting for transfers between devices: 393 us -> 0 us
  Pallas kernels: 0 us -> 99.1 us
  blocking collectives: 73.8 us -> 0 us
  local copies, waits for them, and re-layouts: 39.8 us -> 6.18 us
  matrix products: 18.7 us -> 0 us
  between operations: 15.2 us -> 0.02 us
  other arithmetic: 6.54 us -> 0 us
    all_gather x4 -> x0, waiting for transfers between devices: 393 us -> none  [the longest x1 134 us: local(): lax.all_gather(left, 'col', axis=1, tiled=True)]
    pallas_call x0 -> x1, Pallas kernels: none -> 99.1 us  [local(): pl.pallas_call(kernel, out_shape=jax.ShapeDtypeStruct((ROWS, COLS, C), BF...]
    all_to_all x1 -> x0, blocking collectives: 73.8 us -> none  [local(): lax.all_to_all(strip, 'row', split_axis=1, concat_axis=0, tiled=True)]
    all_to_all x4 -> x0, local copies, waits for them, and re-layouts: 28 us -> none  [the longest x2 22.2 us: local(): lax.all_to_all(strip, 'col', split_axis=0, concat_axis=1, tiled=True)]
    dot_general x6 -> x0, matrix products: 18.7 us -> none  [the longest x1 7.05 us: local(): jnp.einsum('kih,kjh->ijh', partner, lax.all_gather(right, 'row', axis=0,...]
  transfers between devices with their start and end apart: 5 -> 0, of which waited for: 4 -> 0; matrix products, arithmetic and copies ran while one was open for 2% -> 0% of each run, Pallas kernels for 0% -> 0%
where the time goes in v1:
time: 106 us; the launch traced here: 105 us
  Pallas kernels  99.1 us (93%)
  local copies, waits for them, and re-layouts  6.18 us (6%)
    pallas_call x1, Pallas kernels, local(): pl.pallas_call(kernel, out_shape=jax.ShapeDtypeStruct((ROWS, COLS, C), BF...  99.1 us
    unnamed x15, local copies, waits for them, and re-layouts  6.18 us

profile of v1, /device:TPU:1, one launch (start us, length us, event | category | flops | bytes accessed | tf_op | source)
XLA Modules:
  0.0 105.3 jit_solution(17413633926329002545)
XLA Ops:
  0.0 0.0 copy-start
  0.0 1.0 copy-done
  1.0 0.0 copy-start.1
  1.0 0.9 copy-done.1
  1.9 0.0 copy-start.2
  1.9 0.8 copy-done.2
  2.8 0.0 copy-start.3
  2.8 0.7 copy-done.3
  3.4 0.0 copy-start.4
  3.4 0.7 copy-done.4
  4.1 0.0 copy-start.5
  4.1 0.7 copy-done.5
  4.8 0.0 copy-start.6
  4.8 0.7 copy-done.6
  5.5 99.1 %shard_map.73 = bf16[16,64,128]{2,1,0:T(8,128)(2,1)S(1)} custom-call(bf16[16,64,128]{2,1,0:T(8,128)(2,1)S(1)} %copy-done.1, f32[2,128]{1,0:T(2,128)S(1)} %copy-done.3, f32[2,128]{1,0:T(2,128)S(1)} %copy-done.4, bf16[2,128,640]{2,1,0:T(8,128)(2,1)S(1)} %copy-done, f32[2,128]{1,0:T(2,128)S(1)} %copy-done.5, f32[2,128]{1,0:T(2,128)S(1)} %copy-done.6, ...), custom_call_target="tpu_custom_call" | custom-call | tf_op jit(solution)/shard_map/pallas_call | solution.py:281
  104.6 0.7 copy.9
Async XLA Ops:
  0.0 1.0 copy-start
  1.0 0.9 copy-start.1
  1.9 0.8 copy-start.2
  2.8 0.7 copy-start.3
  3.4 0.7 copy-start.4
  4.1 0.7 copy-start.5
  4.8 0.7 copy-start.6

commit v2 on v1

--- a/solution.py
+++ b/solution.py
@@ -17,6 +17,7 @@
 GROUP = 2
 NG = NZ // GROUP
 STEPS = (0, 1, 7, 2, 6, 3, 5, 4)
+PLANE = (10, 6, 9, 11, 14, 2, 8, 5, 7, 13, 15, 1, 3, 4, 12)
 BACK = (4, 3, 5, 2, 6, 1, 7, 0)
 EPS = 1e-05
 
@@ -42,23 +43,36 @@
 
 
 def kernel(
-    pair, in_gain, in_bias, projection, out_gain, out_bias, out_weight, updated,
+    pair_in, in_gain_in, in_bias_in, projection_in, out_gain_in, out_bias_in, out_weight_in, updated,
+    pair, in_gain, in_bias, projection, out_gain, out_bias, out_weight, s0,
     state, normed, gate, cols, wt, wo,
     sa, ra, spread, sx, rx, am, at, bm, tx, ty, tz, tf,
     s1, r1, s2, r2, s3, r3, s4, r4, s5, r5,
 ):
+    loads = [
+        pltpu.make_async_copy(src, dst, s0.at[i])
+        for i, (src, dst) in enumerate((
+            (pair_in, pair), (projection_in, projection), (in_gain_in, in_gain), (in_bias_in, in_bias),
+            (out_gain_in, out_gain), (out_bias_in, out_bias), (out_weight_in, out_weight),
+        ))
+    ]
+    for load in loads:
+        load.start()
+
     row = lax.axis_index("row")
     col = lax.axis_index("col")
     core = row % 2
     z = (row // 2) % NZ
     yh = row // (2 * NZ)
-    p = col * 2 + yh
+    x = col // 2
+    y = yh * 2 + col % 2
+    p = x * 4 + y
 
     def zdev(zz):
         return ((yh * NZ + zz) * 2 + core, col)
 
     def pdev(pp):
-        return (((pp % 2) * NZ + z) * 2 + core, pp // 2)
+        return (((pp % 4 // 2) * NZ + z) * 2 + core, (pp // 4) * 2 + pp % 2)
 
     sibling = (row - core + (1 - core), col)
 
@@ -68,8 +82,11 @@
         pl.semaphore_signal(barrier, 1, device_id=zdev((z + d) % NZ), device_id_type=pl.DeviceIdType.MESH)
         return 0
 
+    def across(d):
+        return ((x + d // 4) % 4) * 4 + (y + d % 4) % 4
+
     def greet_p(d, _):
-        pl.semaphore_signal(barrier, 1, device_id=pdev((p + d) % NP), device_id_type=pl.DeviceIdType.MESH)
+        pl.semaphore_signal(barrier, 1, device_id=pdev(across(d)), device_id_type=pl.DeviceIdType.MESH)
         return 0
 
     lax.fori_loop(1, NZ, greet_z, 0)
@@ -87,6 +104,8 @@
     def swap(x):
         return pltpu.roll(x, COLS, 1)
 
+    for load in loads:
+        load.wait()
     for t in range(8):
         tile = jnp.concatenate([pair[t], pair[t + 8]], axis=0).astype(F32)
         state[:, t * 128:(t + 1) * 128] = tile.T
@@ -96,8 +115,6 @@
         for g in range(5):
             wt[u, g * 128:(g + 1) * 128, :] = projection[u, :, g * 128:(g + 1) * 128].astype(F32).T.astype(BF16)
         wo[u] = out_weight[u].astype(F32).T.astype(BF16)
-
-    pl.semaphore_wait(barrier, NZ - 1 + NP - 1 + 1)
 
     for u in range(2):
         def project(t, _):
@@ -113,7 +130,9 @@
 
         lax.fori_loop(0, 8, project, 0)
 
-        for d in (4, 3, 5, 2, 6, 1, 7):
+        if u == 0:
+            pl.semaphore_wait(barrier, NZ - 1 + NP - 1 + 1)
+        for d in STEPS[1:]:
             to = (z + d) % NZ
             remote(sa.at[u, to], ra.at[u, z], s1.at[u, d], r1.at[u, z], zdev(to)).start()
 
@@ -138,19 +157,20 @@
 
         def send_plane(g):
             steps = pl.ds(g * GROUP, GROUP)
-            pltpu.make_async_copy(sx.at[u, p, steps], rx.at[u, col, yh, core, steps], r2.at[u, g]).start()
+            rx[u, col, yh, core, steps] = sx[u, p, steps]
 
             def one(d, _):
-                to = (p + d) % NP
+                to = across(d)
                 remote(sx.at[u, to, steps], rx.at[u, col, yh, core, steps], s2.at[u, g], r2.at[u, g], pdev(to)).start()
                 return 0
 
-            lax.fori_loop(1, NP, one, 0)
+            [one(d, 0) for d in PLANE]
 
         def swap_cores(g):
             steps = pl.ds(g * GROUP, GROUP)
             whole = rx.at[u, :, :, core, steps]
-            pltpu.make_async_copy(whole, whole, r2.at[u, g]).wait()
+            part = sx.at[u, pl.ds(0, NP - 1), steps]
+            pltpu.make_async_copy(part, part, r2.at[u, g]).wait()
             remote(whole, whole, s3.at[u, g], r3.at[u, g], sibling).start()
 
         def build(g):
@@ -172,13 +192,10 @@
             for s in range(g * GROUP, (g + 1) * GROUP):
                 spread_out(s)
             send_plane(g)
-            if g > 0:
-                swap_cores(g - 1)
-            if g > 1:
-                build(g - 2)
-        swap_cores(NG - 1)
-        build(NG - 2)
-        build(NG - 1)
+        for g in range(NG):
+            swap_cores(g)
+        for g in range(NG):
+            build(g)
 
         if u == 1:
             def flip(i, _):
@@ -204,22 +221,22 @@
                         block = tri[(s * 2 + h) * 16:(s * 2 + h + 1) * 16, c * 128:(c + 1) * 128]
                         first.append(jnp.where(low, block[0:8], swap(block[8:16])))
                         second.append(jnp.where(low, swap(block[0:8]), block[8:16]))
-                    tx[u, g, 4 * c + h] = jnp.concatenate(first, axis=0).astype(BF16)
-                    tx[u, g, 4 * c + 2 + h] = jnp.concatenate(second, axis=0).astype(BF16)
+                    tx[u, g, 4 * c + 2 * h] = jnp.concatenate(first, axis=0).astype(BF16)
+                    tx[u, g, 4 * c + 2 * h + 1] = jnp.concatenate(second, axis=0).astype(BF16)
 
         def send_back(g):
-            pltpu.make_async_copy(tx.at[u, g, p], ty.at[u, g, p], r4.at[u, g]).start()
+            ty[u, g, p] = tx[u, g, p]
 
             def one(d, _):
-                to = (p + d) % NP
+                to = across(d)
                 remote(tx.at[u, g, to], ty.at[u, g, p], s4.at[u, g], r4.at[u, g], pdev(to)).start()
                 return 0
 
-            lax.fori_loop(1, NP, one, 0)
+            [one(d, 0) for d in PLANE]
 
         def gather_back(g):
-            whole = ty.at[u, g]
-            pltpu.make_async_copy(whole, whole, r4.at[u, g]).wait()
+            part = ty.at[u, g, pl.ds(0, NP - 1)]
+            pltpu.make_async_copy(part, part, r4.at[u, g]).wait()
             for h in range(NP):
                 spread[pl.ds(h, 16, stride=16), :] = ty[u, g, h].astype(F32)
             for n in range(GROUP):
@@ -237,9 +254,8 @@
         for g in range(NG):
             triangle(g)
             send_back(g)
-            if g > 0:
-                gather_back(g - 1)
-        gather_back(NG - 1)
+        for g in range(NG):
+            gather_back(g)
 
         for d in range(1, NZ):
             zs = (z + d) % NZ
@@ -281,9 +297,17 @@
     return pl.pallas_call(
         kernel,
         out_shape=jax.ShapeDtypeStruct((ROWS, COLS, C), BF16),
-        in_specs=[pl.BlockSpec(memory_space=vm)] * 7,
+        in_specs=[pl.BlockSpec(memory_space=pltpu.HBM)] * 7,
         out_specs=pl.BlockSpec(memory_space=vm),
         scratch_shapes=[
+            vm((ROWS, COLS, C), BF16),
+            vm((2, C), F32),
+            vm((2, C), F32),
+            vm((2, C, 640), BF16),
+            vm((2, H), F32),
+            vm((2, H), F32),
+            vm((2, H, C), BF16),
+            dma((7,)),
             vm((C, LANES), F32),
             vm((C, LANES), BF16),
             vm((C, LANES), F32),
@@ -309,7 +333,7 @@
             dma((2, NZ)), dma((2, NZ)),
         ],
         compiler_params=pltpu.CompilerParams(
-            collective_id=0, has_side_effects=True, vmem_limit_bytes=40 * 1024 * 1024
+            collective_id=0, has_side_effects=True, vmem_limit_bytes=62 * 1024 * 1024
         ),
     )(pair, in_gain, in_bias, projection, out_gain, out_bias, out_weight)
 

time: 106 us -> 88.2 us (0.83)
  Pallas kernels: 99.1 us -> 86.4 us
  local copies, waits for them, and re-layouts: 6.18 us -> 1.67 us
    pallas_call x1, Pallas kernels: 99.1 us -> 86.4 us  [local(): pl.pallas_call(kernel, out_shape=jax.ShapeDtypeStruct((ROWS, COLS, C), BF...]
    unnamed x15 -> x1, local copies, waits for them, and re-layouts: 6.18 us -> 1.67 us
where the time goes in v2:
time: 88.2 us; the launch traced here: 88.1 us
  Pallas kernels  86.4 us (98%)
  local copies, waits for them, and re-layouts  1.67 us (2%)
    pallas_call x1, Pallas kernels, local(): pl.pallas_call(kernel, out_shape=jax.ShapeDtypeStruct((ROWS, COLS, C), BF...  86.4 us

profile of v2, /device:TPU:1, one launch (start us, length us, event | category | flops | bytes accessed | tf_op | source)
XLA Modules:
  0.0 88.1 jit_solution(11991799367876268840)
XLA Ops:
  0.0 86.4 %shard_map.73 = bf16[16,64,128]{2,1,0:T(8,128)(2,1)} custom-call(bf16[16,64,128]{2,1,0:T(8,128)(2,1)} %pair_in.1, f32[2,128]{1,0:T(2,128)} %in_gain_in.1, f32[2,128]{1,0:T(2,128)} %in_bias_in.1, bf16[2,128,640]{2,1,0:T(8,128)(2,1)} %projection_in.1, f32[2,128]{1,0:T(2,128)} %out_gain_in.1, f32[2,128]{1,0:T(2,128)} %out_bias_in.1, ...), custom_call_target="tpu_custom_call" | custom-call | tf_op jit(solution)/shard_map/pallas_call | solution.py:297
  86.4 1.7 %copy.9 = bf16[16,64,128]{2,1,0:T(8,128)(2,1)} copy(bf16[16,64,128]{2,1,0:T(8,128)(2,1)} %shard_map.73) | data formatting | bytes 524288

commit v3 on v2

v3 whole, which is shorter than its diff:
```python
import jax
import jax.numpy as jnp
from jax import lax
from jax.experimental import pallas as pl
from jax.experimental.pallas import tpu as pltpu
from jax.sharding import PartitionSpec as P

F32 = jnp.float32
BF16 = jnp.bfloat16
C = 128
H = 128
ROWS = 16
COLS = 64
LANES = ROWS * COLS
NZ = 8
NP = 16
FWD = ((0, 1, 7), (2, 6), (3, 5), (4,))
NF = len(FWD)
SWAP_LAG = 2
GROUP = 2
NG = NZ // GROUP
HALF = LANES // 2
UNROLL = 4
STEPS = sum(FWD, ())
START = tuple(sum(len(f) for f in FWD[:g]) for g in range(NF + 1))


def part(g):
    return pl.ds(START[g], len(FWD[g]))


PLANE = (10, 6, 9, 11, 14, 2, 8, 5, 7, 13, 15, 1, 3, 4, 12)
BACK = (3, 5, 4, 2, 6, 1, 7, 0)
EPS = 1e-05


def column(row):
    eye = lax.broadcasted_iota(jnp.int32, (C, C), 0) == lax.broadcasted_iota(jnp.int32, (C, C), 1)
    return jnp.sum(jnp.where(eye, jnp.broadcast_to(row, (C, C)), 0.0), axis=1, keepdims=True)


def norm0(values, gain, offset):
    mean = jnp.sum(values, axis=0, keepdims=True) * (1.0 / C)
    centred = values - mean
    var = jnp.sum(centred * centred, axis=0, keepdims=True) * (1.0 / C)
    return centred * lax.rsqrt(var + EPS) * gain + offset


def sigmoid(x):
    return 0.5 * jnp.tanh(0.5 * x) + 0.5


def dot(a, b, dims):
    return lax.dot_general(a, b, (dims, ((), ())), preferred_element_type=F32)


def kernel(
    pair_in, in_gain_in, in_bias_in, projection_in, out_gain_in, out_bias_in, out_weight_in, updated,
    pair, in_gain, in_bias, projection, out_gain, out_bias, out_weight, s0,
    state, normed, gate, cols, wt, wo,
    sa, ra, spread, sx, rx, am, at, bm, ts, tx, ty, spread2, tz, tf,
    s1, r1, s2, r2, s3, r3, s4, r4, s5, r5,
):
    loads = [
        pltpu.make_async_copy(src, dst, s0.at[i])
        for i, (src, dst) in enumerate((
            (pair_in, pair), (projection_in, projection), (in_gain_in, in_gain), (in_bias_in, in_bias),
            (out_gain_in, out_gain), (out_bias_in, out_bias), (out_weight_in, out_weight),
        ))
    ]
    for load in loads:
        load.start()

    row = lax.axis_index("row")
    col = lax.axis_index("col")
    core = row % 2
    z = (row // 2) % NZ
    yh = row // (2 * NZ)
    x = col // 2
    y = yh * 2 + col % 2
    p = x * 4 + y

    def zdev(zz):
        return ((yh * NZ + zz) * 2 + core, col)

    def pdev(pp):
        return (((pp % 4 // 2) * NZ + z) * 2 + core, (pp // 4) * 2 + pp % 2)

    sibling = (row - core + (1 - core), col)

    barrier = pltpu.get_barrier_semaphore()

    def greet_z(d, _):
        pl.semaphore_signal(barrier, 1, device_id=zdev((z + d) % NZ), device_id_type=pl.DeviceIdType.MESH)
        return 0

    def across(d):
        return ((x + d // 4) % 4) * 4 + (y + d % 4) % 4

    def greet_p(d, _):
        pl.semaphore_signal(barrier, 1, device_id=pdev(across(d)), device_id_type=pl.DeviceIdType.MESH)
        return 0

    lax.fori_loop(1, NZ, greet_z, 0)
    lax.fori_loop(1, NP, greet_p, 0)
    pl.semaphore_signal(barrier, 1, device_id=sibling, device_id_type=pl.DeviceIdType.MESH)

    def remote(src, dst, send, recv, device):
        return pltpu.make_async_remote_copy(
            src_ref=src, dst_ref=dst, send_sem=send, recv_sem=recv,
            device_id=device, device_id_type=pl.DeviceIdType.MESH,
        )

    low = lax.broadcasted_iota(jnp.int32, (1, 128), 1) < COLS

    def swap(x):
        return pltpu.roll(x, COLS, 1)

    for load in loads:
        load.wait()
    for t in range(8):
        tile = jnp.concatenate([pair[t], pair[t + 8]], axis=0).astype(F32)
        state[:, t * 128:(t + 1) * 128] = tile.T
    for u in range(2):
        for n, ref in enumerate((in_gain, in_bias, out_gain, out_bias)):
            cols[u, n] = jnp.broadcast_to(column(ref[u:u + 1, :]), (C, 128))
        for g in range(5):
            wt[u, g * 128:(g + 1) * 128, :] = projection[u, :, g * 128:(g + 1) * 128].astype(F32).T.astype(BF16)
        wo[u] = out_weight[u].astype(F32).T.astype(BF16)

    def project(u, half):
        def one(t, _):
            lanes = pl.ds(pl.multiple_of((half * 4 + t) * 128, 128), 128)
            part_lanes = pl.ds(pl.multiple_of(t * 128, 128), 128)
            nrm = norm0(state[:, lanes], cols[u, 0], cols[u, 1]).astype(BF16)
            normed[:, lanes] = nrm
            proj = dot(wt[u, :512, :], nrm, ((1,), (0,)))
            left = (sigmoid(proj[128:256]) * proj[:128]).astype(BF16)
            right = (sigmoid(proj[384:512]) * proj[256:384]).astype(BF16)
            sa[u, half, :, 0:16, part_lanes] = left.reshape(NZ, 16, 128)
            sa[u, half, :, 16:32, part_lanes] = right.reshape(NZ, 16, 128)
            return 0

        lax.fori_loop(0, 4, one, 0, unroll=UNROLL)

    def send_z(u, half):
        for d in STEPS[1:]:
            to = (z + d) % NZ
            remote(sa.at[u, half, to], ra.at[u, half, z], s1.at[u, half, d], r1.at[u, half, z], zdev(to)).start()

    project(0, 0)
    pl.semaphore_wait(barrier, NZ - 1 + NP - 1 + 1)
    send_z(0, 0)
    project(0, 1)
    send_z(0, 1)

    for u in range(2):
        def gates(t, _):
            lanes = pl.ds(pl.multiple_of(t * 128, 128), 128)
            gate[:, lanes] = sigmoid(dot(wt[u, 512:, :], normed[:, lanes], ((1,), (0,))))
            return 0

        lax.fori_loop(0, 8, gates, 0, unroll=UNROLL)

        def spread_out(s):
            zs = (z + STEPS[s]) % NZ
            for half in range(2):
                if s > 0:
                    remote(sa.at[u, half, zs], ra.at[u, half, zs], s1.at[u, half, 0], r1.at[u, half, zs], zdev(zs)).wait_recv()
                src = sa.at[u, half, zs] if s == 0 else ra.at[u, half, zs]
                for t in range(4):
                    vl = src[0:16, t * 128:(t + 1) * 128].astype(F32)
                    vr = src[16:32, t * 128:(t + 1) * 128].astype(F32)
                    n = half * 4 + t
                    spread[pl.ds(n, 16, stride=16), :] = jnp.where(low, vl, swap(vr))
                    spread[pl.ds(8 + n, 16, stride=16), :] = jnp.where(low, swap(vl), vr)
            sx[u, :, s] = spread[...].reshape(NP, 16, 128).astype(BF16)

        def send_plane(g):
            steps = part(g)
            rx[u, col, yh, core, steps] = sx[u, p, steps]

            def one(d, _):
                to = across(d)
                remote(sx.at[u, to, steps], rx.at[u, col, yh, core, steps], s2.at[u, g], r2.at[u, g], pdev(to)).start()
                return 0

            [one(d, 0) for d in PLANE]

        def swap_cores(g):
            steps = part(g)
            whole = rx.at[u, :, :, core, steps]
            most = sx.at[u, pl.ds(0, NP - 1), steps]
            pltpu.make_async_copy(most, most, r2.at[u, g]).wait()
            remote(whole, whole, s3.at[u, g], r3.at[u, g], sibling).start()

        def build(g):
            steps = part(g)
            other = rx.at[u, :, :, 1 - core, steps]
            pltpu.make_async_copy(other, other, r3.at[u, g]).wait()
            for s in range(START[g], START[g + 1]):
                zs = (z + STEPS[s]) % NZ
                for h in range(2):
                    for k in range(2):
                        place = pl.ds(pl.multiple_of(((h * NZ + zs) * 2 + k) * 16, 16), 16)
                        for c in range(4):
                            x0 = rx[u, 2 * c, h, k, s].astype(F32)
                            x1 = rx[u, 2 * c + 1, h, k, s].astype(F32)
                            am[place, c * 128:(c + 1) * 128] = jnp.where(low, x0, swap(x1)).astype(BF16)
                            bm[place, c * 128:(c + 1) * 128] = jnp.where(low, swap(x0), x1).astype(BF16)

        for g in range(NF):
            for s in range(START[g], START[g + 1]):
                spread_out(s)
            send_plane(g)
            if g >= SWAP_LAG:
                swap_cores(g - SWAP_LAG)
        for g in range(max(0, NF - SWAP_LAG), NF):
            swap_cores(g)
        for g in range(NF):
            build(g)

        if u == 1:
            def flip(i, _):
                lanes = pl.ds(pl.multiple_of(i * 128, 128), 128)
                for k in range(4):
                    at[lanes, k * 128:(k + 1) * 128] = am[k * 128:(k + 1) * 128, lanes].astype(F32).T.astype(BF16)
                return 0

            lax.fori_loop(0, 4, flip, 0)
        a_ref = am if u == 0 else at

        def triangle(g):
            rows = []
            for s in BACK[g * GROUP:(g + 1) * GROUP]:
                for h in range(2):
                    r = ((h * NZ + (z + s) % NZ) * 2 + core) * 16
                    rows.append(a_ref[pl.ds(pl.multiple_of(r, 16), 16), :])
            tri = dot(jnp.concatenate(rows, axis=0), bm[...], ((1,), (1 - u,)))
            for n in range(GROUP):
                for h in range(2):
                    for c in range(4):
                        block = tri[(n * 2 + h) * 16:(n * 2 + h + 1) * 16, c * 128:(c + 1) * 128]
                        first = jnp.where(low, block[0:8], swap(block[8:16]))
                        second = jnp.where(low, swap(block[0:8]), block[8:16])
                        at_row = (g * GROUP + n) * 4
                        for half in range(2):
                            rows4 = slice(half * 4, half * 4 + 4)
                            ts[half, 4 * c + 2 * h, at_row:at_row + 4] = first[rows4]
                            ts[half, 4 * c + 2 * h + 1, at_row:at_row + 4] = second[rows4]

        def send_back(half):
            tx[u, half] = ts[half].astype(BF16)
            for d in PLANE:
                to = across(d)
                remote(tx.at[u, half, to], ty.at[u, half, p], s4.at[u, half], r4.at[u, half], pdev(to)).start()
            ty[u, half, p] = tx[u, half, p]

        def gather_back(half):
            most = ty.at[u, half, pl.ds(0, NP - 1)]
            pltpu.make_async_copy(most, most, r4.at[u, half]).wait()
            for h in range(NP):
                spread2[pl.ds(h, 32, stride=16), :] = ty[u, half, h].astype(F32)
            for n in range(NZ):
                d = BACK[n]
                for t in range(4):
                    at_row = (n * 4 + t) * 16
                    tile = spread2[at_row:at_row + 16, :].astype(BF16)
                    if d == 0:
                        tf[u, half, z, :, t * 128:(t + 1) * 128] = tile
                    else:
                        tz[u, half, d, :, t * 128:(t + 1) * 128] = tile
                if d:
                    remote(tz.at[u, half, d], tf.at[u, half, z], s5.at[u, half, d], r5.at[u, half, z], zdev((z + d) % NZ)).start()

        def wait_back(half):
            for d in range(1, NZ):
                zs = (z + d) % NZ
                remote(tz.at[u, half, d], tf.at[u, half, zs], s5.at[u, half, d], r5.at[u, half, zs], zdev(zs)).wait_recv()

        def finish(half):
            def one(t, _):
                lanes = pl.ds(pl.multiple_of((half * 4 + t) * 128, 128), 128)
                tri = tf[u, half, :, :, pl.ds(pl.multiple_of(t * 128, 128), 128)].reshape(H, 128).astype(F32)
                nrm = norm0(tri, cols[u, 2], cols[u, 3]).astype(BF16)
                delta = dot(wo[u], nrm, ((1,), (0,)))
                new = state[:, lanes] + gate[:, lanes] * delta
                if u == 0:
                    state[:, lanes] = new.astype(BF16).astype(F32)
                else:
                    tile = new.T.astype(BF16)
                    updated[half * 4 + t] = tile[0:COLS]
                    updated[half * 4 + t + 8] = tile[COLS:]
                return 0

            lax.fori_loop(0, 4, one, 0, unroll=UNROLL)

        for g in range(NG):
            triangle(g)
        for half in range(2):
            send_back(half)
        for half in range(2):
            gather_back(half)
        for half in range(2):
            wait_back(half)
            finish(half)
            if u == 0:
                project(1, half)
                send_z(1, half)

    for u in range(2):
        for half in range(2):
            for d in range(1, NZ):
                zs = (z + d) % NZ
                remote(sa.at[u, half, zs], ra.at[u, half, z], s1.at[u, half, d], r1.at[u, half, z], zdev(zs)).wait_send()
                remote(tz.at[u, half, d], tf.at[u, half, z], s5.at[u, half, d], r5.at[u, half, z], zdev(zs)).wait_send()
            sent = tx.at[u, half, pl.ds(0, NP - 1)]
            pltpu.make_async_copy(sent, sent, s4.at[u, half]).wait()
        for g in range(NF):
            sent = sx.at[u, pl.ds(0, NP - 1), part(g)]
            pltpu.make_async_copy(sent, sent, s2.at[u, g]).wait()
            sent = rx.at[u, :, :, core, part(g)]
            pltpu.make_async_copy(sent, sent, s3.at[u, g]).wait()


def local(pair, in_gain, in_bias, projection, out_gain, out_bias, out_weight):
    vm = pltpu.VMEM
    dma = pltpu.SemaphoreType.DMA
    return pl.pallas_call(
        kernel,
        out_shape=jax.ShapeDtypeStruct((ROWS, COLS, C), BF16),
        in_specs=[pl.BlockSpec(memory_space=pltpu.HBM)] * 7,
        out_specs=pl.BlockSpec(memory_space=vm),
        scratch_shapes=[
            vm((ROWS, COLS, C), BF16),
            vm((2, C), F32),
            vm((2, C), F32),
            vm((2, C, 640), BF16),
            vm((2, H), F32),
            vm((2, H), F32),
            vm((2, H, C), BF16),
            dma((7,)),
            vm((C, LANES), F32),
            vm((C, LANES), BF16),
            vm((C, LANES), F32),
            vm((2, 4, C, 128), F32),
            vm((2, 640, C), BF16),
            vm((2, C, H), BF16),
            vm((2, 2, NZ, 32, HALF), BF16),
            vm((2, 2, NZ, 32, HALF), BF16),
            vm((256, 128), F32),
            vm((2, NP, NZ, 16, 128), BF16),
            vm((2, 8, 2, 2, NZ, 16, 128), BF16),
            vm((512, 512), BF16),
            vm((512, 512), BF16),
            vm((512, 512), BF16),
            vm((2, NP, 32, 128), F32),
            vm((2, 2, NP, 32, 128), BF16),
            vm((2, 2, NP, 32, 128), BF16),
            vm((512, 128), F32),
            vm((2, 2, NZ, 16, HALF), BF16),
            vm((2, 2, NZ, 16, HALF), BF16),
            dma((2, 2, NZ)), dma((2, 2, NZ)),
            dma((2, NF)), dma((2, NF)),
            dma((2, NF)), dma((2, NF)),
            dma((2, 2)), dma((2, 2)),
            dma((2, 2, NZ)), dma((2, 2, NZ)),
        ],
        compiler_params=pltpu.CompilerParams(
            collective_id=0, has_side_effects=True, vmem_limit_bytes=62 * 1024 * 1024
        ),
    )(pair, in_gain, in_bias, projection, out_gain, out_bias, out_weight)


def solution(mesh):
    return jax.shard_map(
        local,
        mesh=mesh,
        in_specs=(P("row", "col", None), P(), P(), P(), P(), P(), P()),
        out_specs=P("row", "col", None),
        check_vma=False,
    )
```

time: 88.2 us -> 84.4 us (0.957)
  Pallas kernels: 86.4 us -> 82.6 us
    pallas_call x1, Pallas kernels: 86.4 us -> 82.6 us  [local(): pl.pallas_call(kernel, out_shape=jax.ShapeDtypeStruct((ROWS, COLS, C), BF...]
where the time goes in v3:
time: 84.4 us; the launch traced here: 84.3 us
  Pallas kernels  82.6 us (98%)
  local copies, waits for them, and re-layouts  1.67 us (2%)
    pallas_call x1, Pallas kernels, local(): pl.pallas_call(kernel, out_shape=jax.ShapeDtypeStruct((ROWS, COLS, C), BF...  82.6 us

profile of v3, /device:TPU:1, one launch (start us, length us, event | category | flops | bytes accessed | tf_op | source)
XLA Modules:
  0.0 84.3 jit_solution(8817223531505112370)
XLA Ops:
  0.0 82.6 %shard_map.73 = bf16[16,64,128]{2,1,0:T(8,128)(2,1)} custom-call(bf16[16,64,128]{2,1,0:T(8,128)(2,1)} %pair_in.1, f32[2,128]{1,0:T(2,128)} %in_gain_in.1, f32[2,128]{1,0:T(2,128)} %in_bias_in.1, bf16[2,128,640]{2,1,0:T(8,128)(2,1)} %projection_in.1, f32[2,128]{1,0:T(2,128)} %out_gain_in.1, f32[2,128]{1,0:T(2,128)} %out_bias_in.1, ...), custom_call_target="tpu_custom_call" | custom-call | tf_op jit(solution)/shard_map/pallas_call | solution.py:329
  82.6 1.7 %copy.9 = bf16[16,64,128]{2,1,0:T(8,128)(2,1)} copy(bf16[16,64,128]{2,1,0:T(8,128)(2,1)} %shard_map.73) | data formatting | bytes 524288

commit v4 on v3

--- a/solution.py
+++ b/solution.py
@@ -16,7 +16,7 @@
 NP = 16
 FWD = ((0, 1, 7), (2, 6), (3, 5), (4,))
 NF = len(FWD)
-SWAP_LAG = 2
+SWAP_LAG = 3
 GROUP = 2
 NG = NZ // GROUP
 HALF = LANES // 2
@@ -86,6 +86,9 @@
     def pdev(pp):
         return (((pp % 4 // 2) * NZ + z) * 2 + core, (pp // 4) * 2 + pp % 2)
 
+    def twin(pp):
+        return (((pp % 4 // 2) * NZ + z) * 2 + (1 - core), (pp // 4) * 2 + pp % 2)
+
     sibling = (row - core + (1 - core), col)
 
     barrier = pltpu.get_barrier_semaphore()
@@ -99,6 +102,7 @@
 
     def greet_p(d, _):
         pl.semaphore_signal(barrier, 1, device_id=pdev(across(d)), device_id_type=pl.DeviceIdType.MESH)
+        pl.semaphore_signal(barrier, 1, device_id=twin(across(d)), device_id_type=pl.DeviceIdType.MESH)
         return 0
 
     lax.fori_loop(1, NZ, greet_z, 0)
@@ -149,7 +153,7 @@
             remote(sa.at[u, half, to], ra.at[u, half, z], s1.at[u, half, d], r1.at[u, half, z], zdev(to)).start()
 
     project(0, 0)
-    pl.semaphore_wait(barrier, NZ - 1 + NP - 1 + 1)
+    pl.semaphore_wait(barrier, NZ - 1 + 2 * (NP - 1) + 1)
     send_z(0, 0)
     project(0, 1)
     send_z(0, 1)
@@ -178,21 +182,23 @@
 
         def send_plane(g):
             steps = part(g)
+            here = (u, col, yh, core, steps)
+            for d in PLANE:
+                to = across(d)
+                if g == NF - 1:
+                    remote(sx.at[u, to, steps], rx.at[here], s3.at[u, g], r3.at[u, g], twin(to)).start()
+                remote(sx.at[u, to, steps], rx.at[here], s2.at[u, g], r2.at[u, g], pdev(to)).start()
+            if g == NF - 1:
+                remote(sx.at[u, p, steps], rx.at[here], s3.at[u, g], r3.at[u, g], sibling).start()
             rx[u, col, yh, core, steps] = sx[u, p, steps]
-
-            def one(d, _):
-                to = across(d)
-                remote(sx.at[u, to, steps], rx.at[u, col, yh, core, steps], s2.at[u, g], r2.at[u, g], pdev(to)).start()
-                return 0
-
-            [one(d, 0) for d in PLANE]
 
         def swap_cores(g):
             steps = part(g)
             whole = rx.at[u, :, :, core, steps]
             most = sx.at[u, pl.ds(0, NP - 1), steps]
             pltpu.make_async_copy(most, most, r2.at[u, g]).wait()
-            remote(whole, whole, s3.at[u, g], r3.at[u, g], sibling).start()
+            if g < NF - 1:
+                remote(whole, whole, s3.at[u, g], r3.at[u, g], sibling).start()
 
         def build(g):
             steps = part(g)
@@ -215,8 +221,9 @@
             send_plane(g)
             if g >= SWAP_LAG:
                 swap_cores(g - SWAP_LAG)
-        for g in range(max(0, NF - SWAP_LAG), NF):
+        for g in range(max(0, NF - SWAP_LAG), NF - 1):
             swap_cores(g)
+        swap_cores(NF - 1)
         for g in range(NF):
             build(g)
 
@@ -319,7 +326,7 @@
         for g in range(NF):
             sent = sx.at[u, pl.ds(0, NP - 1), part(g)]
             pltpu.make_async_copy(sent, sent, s2.at[u, g]).wait()
-            sent = rx.at[u, :, :, core, part(g)]
+            sent = sx.at[u, :, part(g)] if g == NF - 1 else rx.at[u, :, :, core, part(g)]
             pltpu.make_async_copy(sent, sent, s3.at[u, g]).wait()
 
 

time: 84.4 us -> 81.8 us (0.969)
  Pallas kernels: 82.6 us -> 80 us
    pallas_call x1, Pallas kernels: 82.6 us -> 80 us  [local(): pl.pallas_call(kernel, out_shape=jax.ShapeDtypeStruct((ROWS, COLS, C), BF...]
where the time goes in v4:
time: 81.8 us; the launch traced here: 81.7 us
  Pallas kernels  80 us (98%)
  local copies, waits for them, and re-layouts  1.67 us (2%)
    pallas_call x1, Pallas kernels, local(): pl.pallas_call(kernel, out_shape=jax.ShapeDtypeStruct((ROWS, COLS, C), BF...  80 us
    unnamed x1, local copies, waits for them, and re-layouts  1.67 us

profile of v4, /device:TPU:1, one launch (start us, length us, event | category | flops | bytes accessed | tf_op | source)
XLA Modules:
  0.0 81.7 jit_solution(16613859018104216985)
XLA Ops:
  0.0 80.0 %shard_map.73 = bf16[16,64,128]{2,1,0:T(8,128)(2,1)} custom-call(bf16[16,64,128]{2,1,0:T(8,128)(2,1)} %pair_in.1, f32[2,128]{1,0:T(2,128)} %in_gain_in.1, f32[2,128]{1,0:T(2,128)} %in_bias_in.1, bf16[2,128,640]{2,1,0:T(8,128)(2,1)} %projection_in.1, f32[2,128]{1,0:T(2,128)} %out_gain_in.1, f32[2,128]{1,0:T(2,128)} %out_bias_in.1, ...), custom_call_target="tpu_custom_call" | custom-call | tf_op jit(solution)/shard_map/pallas_call | solution.py:336
  80.0 1.7 %copy.9 = bf16[16,64,128]{2,1,0:T(8,128)(2,1)} copy(bf16[16,64,128]{2,1,0:T(8,128)(2,1)} %shard_map.73) | data formatting | bytes 524288

commit v5 on v4

--- a/solution.py
+++ b/solution.py
@@ -73,41 +73,45 @@
 
     row = lax.axis_index("row")
     col = lax.axis_index("col")
-    core = row % 2
-    z = (row // 2) % NZ
-    yh = row // (2 * NZ)
-    x = col // 2
-    y = yh * 2 + col % 2
+    core = lax.rem(row, 2)
+    z = lax.rem(lax.div(row, 2), NZ)
+    yh = lax.div(row, 2 * NZ)
+    x = lax.div(col, 2)
+    y = yh * 2 + lax.rem(col, 2)
     p = x * 4 + y
-
-    def zdev(zz):
-        return ((yh * NZ + zz) * 2 + core, col)
-
-    def pdev(pp):
-        return (((pp % 4 // 2) * NZ + z) * 2 + core, (pp // 4) * 2 + pp % 2)
-
-    def twin(pp):
-        return (((pp % 4 // 2) * NZ + z) * 2 + (1 - core), (pp // 4) * 2 + pp % 2)
-
-    sibling = (row - core + (1 - core), col)
+    other = 1 - core
+    ring_z = [z] + [lax.rem(z + d, NZ) for d in range(1, NZ)]
+    ring_x = [x] + [lax.rem(x + d, 4) for d in range(1, 4)]
+    ring_y = [y] + [lax.rem(y + d, 4) for d in range(1, 4)]
+    row_y = [(lax.div(v, 2) * NZ + z) * 2 for v in ring_y]
+    col_y = [lax.rem(v, 2) for v in ring_y]
+    yh_row = yh * (2 * NZ) + core
+
+    def zdev(d):
+        return (ring_z[d] * 2 + yh_row, col)
+
+    def across(d):
+        return ring_x[d // 4] * 4 + ring_y[d % 4]
+
+    def pdev(d):
+        return (row_y[d % 4] + core, ring_x[d // 4] * 2 + col_y[d % 4])
+
+    def twin(d):
+        return (row_y[d % 4] + other, ring_x[d // 4] * 2 + col_y[d % 4])
+
+    sibling = (row - core + other, col)
 
     barrier = pltpu.get_barrier_semaphore()
 
-    def greet_z(d, _):
-        pl.semaphore_signal(barrier, 1, device_id=zdev((z + d) % NZ), device_id_type=pl.DeviceIdType.MESH)
-        return 0
-
-    def across(d):
-        return ((x + d // 4) % 4) * 4 + (y + d % 4) % 4
-
-    def greet_p(d, _):
-        pl.semaphore_signal(barrier, 1, device_id=pdev(across(d)), device_id_type=pl.DeviceIdType.MESH)
-        pl.semaphore_signal(barrier, 1, device_id=twin(across(d)), device_id_type=pl.DeviceIdType.MESH)
-        return 0
-
-    lax.fori_loop(1, NZ, greet_z, 0)
-    lax.fori_loop(1, NP, greet_p, 0)
-    pl.semaphore_signal(barrier, 1, device_id=sibling, device_id_type=pl.DeviceIdType.MESH)
+    def greet(device):
+        pl.semaphore_signal(barrier, 1, device_id=device, device_id_type=pl.DeviceIdType.MESH)
+
+    for d in (4, 3, 5, 2, 6, 1, 7):
+        greet(zdev(d))
+    for d in PLANE:
+        greet(pdev(d))
+        greet(twin(d))
+    greet(sibling)
 
     def remote(src, dst, send, recv, device):
         return pltpu.make_async_remote_copy(
@@ -149,8 +153,8 @@
 
     def send_z(u, half):
         for d in STEPS[1:]:
-            to = (z + d) % NZ
-            remote(sa.at[u, half, to], ra.at[u, half, z], s1.at[u, half, d], r1.at[u, half, z], zdev(to)).start()
+            to = ring_z[d]
+            remote(sa.at[u, half, to], ra.at[u, half, z], s1.at[u, half, d], r1.at[u, half, z], zdev(d)).start()
 
     project(0, 0)
     pl.semaphore_wait(barrier, NZ - 1 + 2 * (NP - 1) + 1)
@@ -167,10 +171,10 @@
         lax.fori_loop(0, 8, gates, 0, unroll=UNROLL)
 
         def spread_out(s):
-            zs = (z + STEPS[s]) % NZ
+            zs = ring_z[STEPS[s]]
             for half in range(2):
                 if s > 0:
-                    remote(sa.at[u, half, zs], ra.at[u, half, zs], s1.at[u, half, 0], r1.at[u, half, zs], zdev(zs)).wait_recv()
+                    remote(sa.at[u, half, zs], ra.at[u, half, zs], s1.at[u, half, 0], r1.at[u, half, zs], zdev(STEPS[s])).wait_recv()
                 src = sa.at[u, half, zs] if s == 0 else ra.at[u, half, zs]
                 for t in range(4):
                     vl = src[0:16, t * 128:(t + 1) * 128].astype(F32)
@@ -186,8 +190,8 @@
             for d in PLANE:
                 to = across(d)
                 if g == NF - 1:
-                    remote(sx.at[u, to, steps], rx.at[here], s3.at[u, g], r3.at[u, g], twin(to)).start()
-                remote(sx.at[u, to, steps], rx.at[here], s2.at[u, g], r2.at[u, g], pdev(to)).start()
+                    remote(sx.at[u, to, steps], rx.at[here], s3.at[u, g], r3.at[u, g], twin(d)).start()
+                remote(sx.at[u, to, steps], rx.at[here], s2.at[u, g], r2.at[u, g], pdev(d)).start()
             if g == NF - 1:
                 remote(sx.at[u, p, steps], rx.at[here], s3.at[u, g], r3.at[u, g], sibling).start()
             rx[u, col, yh, core, steps] = sx[u, p, steps]
@@ -202,10 +206,10 @@
 
         def build(g):
             steps = part(g)
-            other = rx.at[u, :, :, 1 - core, steps]
-            pltpu.make_async_copy(other, other, r3.at[u, g]).wait()
+            theirs = rx.at[u, :, :, 1 - core, steps]
+            pltpu.make_async_copy(theirs, theirs, r3.at[u, g]).wait()
             for s in range(START[g], START[g + 1]):
-                zs = (z + STEPS[s]) % NZ
+                zs = ring_z[STEPS[s]]
                 for h in range(2):
                     for k in range(2):
                         place = pl.ds(pl.multiple_of(((h * NZ + zs) * 2 + k) * 16, 16), 16)
@@ -241,7 +245,7 @@
             rows = []
             for s in BACK[g * GROUP:(g + 1) * GROUP]:
                 for h in range(2):
-                    r = ((h * NZ + (z + s) % NZ) * 2 + core) * 16
+                    r = ((h * NZ + ring_z[s]) * 2 + core) * 16
                     rows.append(a_ref[pl.ds(pl.multiple_of(r, 16), 16), :])
             tri = dot(jnp.concatenate(rows, axis=0), bm[...], ((1,), (1 - u,)))
             for n in range(GROUP):
@@ -260,7 +264,7 @@
             tx[u, half] = ts[half].astype(BF16)
             for d in PLANE:
                 to = across(d)
-                remote(tx.at[u, half, to], ty.at[u, half, p], s4.at[u, half], r4.at[u, half], pdev(to)).start()
+                remote(tx.at[u, half, to], ty.at[u, half, p], s4.at[u, half], r4.at[u, half], pdev(d)).start()
             ty[u, half, p] = tx[u, half, p]
 
         def gather_back(half):
@@ -278,12 +282,12 @@
                     else:
                         tz[u, half, d, :, t * 128:(t + 1) * 128] = tile
                 if d:
-                    remote(tz.at[u, half, d], tf.at[u, half, z], s5.at[u, half, d], r5.at[u, half, z], zdev((z + d) % NZ)).start()
+                    remote(tz.at[u, half, d], tf.at[u, half, z], s5.at[u, half, d], r5.at[u, half, z], zdev(d)).start()
 
         def wait_back(half):
             for d in range(1, NZ):
-                zs = (z + d) % NZ
-                remote(tz.at[u, half, d], tf.at[u, half, zs], s5.at[u, half, d], r5.at[u, half, zs], zdev(zs)).wait_recv()
+                zs = ring_z[d]
+                remote(tz.at[u, half, d], tf.at[u, half, zs], s5.at[u, half, d], r5.at[u, half, zs], zdev(d)).wait_recv()
 
         def finish(half):
             def one(t, _):
@@ -318,9 +322,9 @@
     for u in range(2):
         for half in range(2):
             for d in range(1, NZ):
-                zs = (z + d) % NZ
-                remote(sa.at[u, half, zs], ra.at[u, half, z], s1.at[u, half, d], r1.at[u, half, z], zdev(zs)).wait_send()
-                remote(tz.at[u, half, d], tf.at[u, half, z], s5.at[u, half, d], r5.at[u, half, z], zdev(zs)).wait_send()
+                zs = ring_z[d]
+                remote(sa.at[u, half, zs], ra.at[u, half, z], s1.at[u, half, d], r1.at[u, half, z], zdev(d)).wait_send()
+                remote(tz.at[u, half, d], tf.at[u, half, z], s5.at[u, half, d], r5.at[u, half, z], zdev(d)).wait_send()
             sent = tx.at[u, half, pl.ds(0, NP - 1)]
             pltpu.make_async_copy(sent, sent, s4.at[u, half]).wait()
         for g in range(NF):

time: 81.8 us -> 79.9 us (0.977)
  Pallas kernels: 80 us -> 78.1 us
    pallas_call x1, Pallas kernels: 80 us -> 78.1 us  [local(): pl.pallas_call(kernel, out_shape=jax.ShapeDtypeStruct((ROWS, COLS, C), BF...]
where the time goes in v5:
time: 79.9 us; the launch traced here: 79.8 us
  Pallas kernels  78.1 us (98%)
  local copies, waits for them, and re-layouts  1.67 us (2%)
    pallas_call x1, Pallas kernels, local(): pl.pallas_call(kernel, out_shape=jax.ShapeDtypeStruct((ROWS, COLS, C), BF...  78.1 us
    unnamed x1, local copies, waits for them, and re-layouts  1.67 us

profile of v5, /device:TPU:1, one launch (start us, length us, event | category | flops | bytes accessed | tf_op | source)
XLA Modules:
  0.0 79.8 jit_solution(17177510525256560718)
XLA Ops:
  0.0 78.1 %shard_map.73 = bf16[16,64,128]{2,1,0:T(8,128)(2,1)} custom-call(bf16[16,64,128]{2,1,0:T(8,128)(2,1)} %pair_in.1, f32[2,128]{1,0:T(2,128)} %in_gain_in.1, f32[2,128]{1,0:T(2,128)} %in_bias_in.1, bf16[2,128,640]{2,1,0:T(8,128)(2,1)} %projection_in.1, f32[2,128]{1,0:T(2,128)} %out_gain_in.1, f32[2,128]{1,0:T(2,128)} %out_bias_in.1, ...), custom_call_target="tpu_custom_call" | custom-call | tf_op jit(solution)/shard_map/pallas_call | solution.py:340
  78.1 1.7 %copy.9 = bf16[16,64,128]{2,1,0:T(8,128)(2,1)} copy(bf16[16,64,128]{2,1,0:T(8,128)(2,1)} %shard_map.73) | data formatting | bytes 524288
